TPU v7x, 32 devices: a whole 2x2x4 slice. The times are simulated.
32 devices in a mesh: orig: 8 (over z, y), dest: 4 (over x, core).
Axes of the slice: x: 2, y: 2, z: 4, core: 2. Of those that a mesh axis runs over, the one named last changes fastest.
Arguments:
- skim_tables: bfloat16 [8, 8192, 8192], P(None, 'orig', 'dest'), may hold values from 0 to 4
- block_scale: float32 [8, 64, 64], P(None, 'orig', 'dest'), may hold values from 0.25 to 60
- mode_coef: float32 [12, 8], replicated, may hold values from -1.2 to 1.2
- mode_const: float32 [12], replicated, may hold values from -4 to 4
- nest_theta: float32 [4], replicated, may hold values from 0.3 to 1
- mode_nest: int32 [12], replicated, may hold values from 0 to 3, as said below
- logsum_coef: float32 [1], replicated, may hold values from 0.5 to 1
- tour_attr: bfloat16 [32768, 128], P('orig')
- zone_attr: bfloat16 [128, 8192], P(None, 'dest')
- block_zone: int32 [1024], P('orig'), may hold values from 0 to 8191, as said below
- block_count: int32 [1024], P('orig'), may hold values from 1 to 32, as said below
Outputs:
- logsums: float32 [8192, 8192], P('orig', 'dest')
- trip_matrix: float32 [8192, 8192], P('orig', 'dest')
Inputs may be any that keep to these rules, and one draw needn't show every extreme that they name: `block_zone`: among the 128 blocks of each aligned run (the blocks of one index of orig), at most 32 have home zones in any one range of 1024 zones (zone // 1024); one range has exactly 32 blocks in every run. `block_count`: each aligned run of 128 blocks has a block with 32 live tours. `mode_nest`: every nest holds at least one mode.
All inputs are finite; a program needn't handle non-finite values.
Results may differ from a plain program's by a relative error of at most 0.0006.
Values may be sent and summed in bfloat16 or wider, within the bound.
A program may use at most 384 MiB of HBM per device.

v0:
```python
import math

import jax
import jax.numpy as jnp
from jax import lax
from jax.sharding import PartitionSpec as P

neg_fill = -1e30


def nest_logsum(skim_part, scale_part, mode_coef, mode_const, nest_theta, mode_nest):
    tables, row_count, col_count = skim_part.shape
    block_rows = row_count // scale_part.shape[1]
    block_cols = col_count // scale_part.shape[2]
    nest_total = nest_theta.shape[0]
    mode_total = mode_coef.shape[0]
    scaled = skim_part.astype(jnp.float32).reshape(
        tables, scale_part.shape[1], block_rows, scale_part.shape[2], block_cols
    )
    scaled = (scaled * scale_part[:, :, None, :, None]).reshape(tables, row_count, col_count)
    member_table = mode_nest[:, None] == jnp.arange(nest_total, dtype=jnp.int32)[None, :]
    mode_theta = jnp.sum(jnp.where(member_table, nest_theta[None, :], jnp.float32(0.0)), axis=1)
    utils = []
    for mode_index in range(mode_total):
        value = mode_const[mode_index] + mode_coef[mode_index, 0] * scaled[0]
        for table_index in range(1, tables):
            value = value + mode_coef[mode_index, table_index] * scaled[table_index]
        utils.append(value / mode_theta[mode_index])
    scaled_util = jnp.stack(utils)
    maxima = []
    for nest_index in range(nest_total):
        member = (mode_nest == nest_index)[:, None, None]
        maxima.append(jnp.max(jnp.where(member, scaled_util, neg_fill), axis=0))
    nest_values = []
    for nest_index in range(nest_total):
        member = (mode_nest == nest_index)[:, None, None]
        shifted = jnp.where(member, scaled_util - maxima[nest_index][None], neg_fill)
        sum_total = jnp.sum(jnp.exp(shifted), axis=0)
        nest_values.append(nest_theta[nest_index] * (maxima[nest_index] + jnp.log(sum_total)))
    stacked = jnp.stack(nest_values)
    row_max = jnp.max(stacked, axis=0)
    return row_max + jnp.log(jnp.sum(jnp.exp(stacked - row_max), axis=0))


def group_scores(feat_part, home_rows, zone_attr, ls_coef):
    block_num, tour_size, features = feat_part.shape
    product = jnp.dot(
        feat_part.reshape(block_num * tour_size, features),
        zone_attr,
        preferred_element_type=jnp.float32,
    )
    return ls_coef * home_rows[:, None, :] + product.reshape(block_num, tour_size, -1)


def tour_trips(tour_feats, home_rows, live_counts, zone_attr, ls_coef, factor):
    block_num, tour_size, features = tour_feats.shape
    dest_width = home_rows.shape[1]
    group_size = math.gcd(block_num, max(1, 512 // tour_size))
    group_steps = block_num // group_size
    grouped_feats = tour_feats.reshape(group_steps, group_size, tour_size, features)
    grouped_rows = home_rows.reshape(group_steps, group_size, dest_width)
    live_mask = (jnp.arange(tour_size)[None, :] < live_counts[:, None]).astype(jnp.float32)
    live_mask = live_mask.reshape(group_steps, group_size, tour_size)

    def local_max(inputs):
        return jnp.max(group_scores(inputs[0], inputs[1], zone_attr, ls_coef), axis=-1)

    row_max = lax.map(local_max, (grouped_feats, grouped_rows))
    row_max = lax.pmax(row_max.astype(jnp.bfloat16), "dest").astype(row_max.dtype)

    def local_total(inputs):
        scores = group_scores(inputs[0], inputs[1], zone_attr, ls_coef)
        return jnp.sum(jnp.exp(scores - inputs[2][:, :, None]), axis=-1)

    sum_total = lax.map(local_total, (grouped_feats, grouped_rows, row_max))
    sum_total = lax.psum(sum_total, "dest")

    def finish(inputs):
        scores = group_scores(inputs[0], inputs[1], zone_attr, ls_coef)
        shares = jnp.exp(scores - inputs[2][:, :, None]) / inputs[3][:, :, None]
        return jnp.sum(shares * inputs[4][:, :, None], axis=1)

    block_sums = lax.map(finish, (grouped_feats, grouped_rows, row_max, sum_total, live_mask))
    return factor * block_sums.reshape(block_num, dest_width)


def local(
    skim_tables,
    block_scale,
    mode_coef,
    mode_const,
    nest_theta,
    mode_nest,
    logsum_coef,
    tour_attr,
    zone_attr,
    block_zone,
    block_count,
):
    logsums = nest_logsum(skim_tables, block_scale, mode_coef, mode_const, nest_theta, mode_nest)
    sources = lax.axis_size("orig")
    blocks_here = block_zone.shape[0]
    anchors = skim_tables.shape[1]
    tour_size = tour_attr.shape[0] // blocks_here
    features = tour_attr.shape[1]
    capacity = max(2, 2 * blocks_here // sources)
    slot_count = sources * capacity
    factor = anchors * sources / tour_size
    ls_coef = logsum_coef[0]
    source_dev = block_zone // anchors
    local_zone = block_zone - source_dev * anchors
    source_hits = (source_dev[:, None] == jnp.arange(sources)[None, :]).astype(jnp.int32)
    slot_rank = jnp.sum((jnp.cumsum(source_hits, axis=0) - source_hits) * source_hits, axis=1)
    slot_of_block = source_dev * capacity + slot_rank
    slot_match = slot_of_block[None, :] == jnp.arange(slot_count)[:, None]
    filled = jnp.any(slot_match, axis=1)
    block_of_slot = jnp.sum(slot_match.astype(jnp.int32) * jnp.arange(blocks_here)[None, :], axis=1)
    request = jnp.where(filled, local_zone[block_of_slot], 0).reshape(sources, capacity)
    tour_feats = tour_attr.reshape(blocks_here, tour_size, features)
    send_feats = jnp.where(filled[:, None, None], tour_feats[block_of_slot], 0).reshape(
        sources, capacity, tour_size, features
    )
    send_counts = jnp.where(filled, block_count[block_of_slot], 0).reshape(sources, capacity)
    recv_feats, asked_zones, recv_counts = (
        lax.all_to_all(send_feats, "orig", split_axis=0, concat_axis=0, tiled=True),
        lax.all_to_all(request, "orig", split_axis=0, concat_axis=0, tiled=True),
        lax.all_to_all(send_counts, "orig", split_axis=0, concat_axis=0, tiled=True),
    )
    asked_zones = asked_zones.reshape(slot_count)
    home_rows = logsums[asked_zones]
    arrived = tour_trips(
        recv_feats.reshape(slot_count, tour_size, features),
        home_rows,
        recv_counts.reshape(slot_count),
        zone_attr,
        ls_coef,
        factor,
    )
    trip_matrix = jax.ops.segment_sum(arrived, asked_zones, num_segments=anchors)
    return (logsums, trip_matrix)


def solution(mesh):
    return jax.shard_map(
        local,
        mesh=mesh,
        in_specs=(
            P(None, "orig", "dest"),
            P(None, "orig", "dest"),
            P(),
            P(),
            P(),
            P(),
            P(),
            P("orig", None),
            P(None, "dest"),
            P("orig"),
            P("orig"),
        ),
        out_specs=(P("orig", "dest"), P("orig", "dest")),
        check_vma=False,
    )
```

profile of v0, /device:TPU:25, one launch (start us, length us, event | category | flops | bytes accessed | tf_op | source)
XLA Modules:
  0.0 1151.9 jit_solution(4871125382489558734)
XLA Ops:
  7.2 5.5 all-to-all-start
  28.5 32.4 %copy.13 = f32[1024,8,16,128]{3,2,1,0:T(8,128)} copy(bf16[1024,8,16,128]{3,1,2,0:T(8,128)(2,1)} %bitcast.255) | data formatting | bytes 100663296
  62.4 44.3 %broadcast_multiply_fusion = f32[8,8,128,16,128]{4,3,2,1,0:T(8,128)} fusion(f32[8,8,128,16,128]{4,3,2,1,0:T(8,128)} %bitcast.157, f32[8,8,16]{2,1,0:T(8,128)S(1)} %copy-done.3), kind=kLoop, calls=%fused_computation.41 | loop fusion | flops 16777216 | bytes 134221824 | tf_op jit(solution)/shard_map/mul | solution.py:20
  106.7 31.6 %add_divide_fusion.10 = f32[1,8,128,16,128]{4,3,2,1,0:T(8,128)} fusion(f32[]{:T(128)} %bitcast.36, f32[]{:T(128)} %bitcast.35, f32[]{:T(128)} %bitcast.34, f32[]{:T(128)} %bitcast.33, f32[]{:T(128)} %bitcast.32, f32[]{:T(128)} %bitcast.31, f32[]{:T(128)} %bitcast.30, f32[]{:T(128)} %bitcast.29, f32[]{:T(128)} %bitcast.28, f32[]{:T(128)} %bitcast.27, ...), kind=kLoop, calls=%fused_computation.52 | loop fusion | flops 35651584 | bytes 75497512 | tf_op jit(solution)/shard_map/div | solution.py:28
  138.3 9.2 reshape.1951
  147.6 31.7 %add_divide_fusion.11 = f32[1,8,128,16,128]{4,3,2,1,0:T(8,128)} fusion(f32[]{:T(128)} %bitcast.26, f32[]{:T(128)} %bitcast.25, f32[]{:T(128)} %bitcast.24, f32[]{:T(128)} %bitcast.23, f32[]{:T(128)} %bitcast.22, f32[]{:T(128)} %bitcast.21, f32[]{:T(128)} %bitcast.20, f32[]{:T(128)} %bitcast.19, f32[]{:T(128)} %bitcast.18, f32[]{:T(128)} %bitcast.17, ...), kind=kLoop, calls=%fused_computation.53 | loop fusion | flops 35651584 | bytes 75497512 | tf_op jit(solution)/shard_map/div | solution.py:28
  179.2 9.2 reshape.1949
  188.5 7.7 constant_dynamic-update-slice_fusion.11
  196.2 31.6 %add_divide_fusion.9 = f32[1,8,128,16,128]{4,3,2,1,0:T(8,128)} fusion(f32[]{:T(128)} %bitcast.46, f32[]{:T(128)} %bitcast.45, f32[]{:T(128)} %bitcast.44, f32[]{:T(128)} %bitcast.43, f32[]{:T(128)} %bitcast.42, f32[]{:T(128)} %bitcast.41, f32[]{:T(128)} %bitcast.40, f32[]{:T(128)} %bitcast.39, f32[]{:T(128)} %bitcast.38, f32[]{:T(128)} %bitcast.37, ...), kind=kLoop, calls=%fused_computation.51 | loop fusion | flops 35651584 | bytes 75497512 | tf_op jit(solution)/shard_map/div | solution.py:28
  227.8 9.2 reshape.1953
  237.0 31.6 %add_divide_fusion.8 = f32[1,8,128,16,128]{4,3,2,1,0:T(8,128)} fusion(f32[]{:T(128)} %bitcast.56, f32[]{:T(128)} %bitcast.55, f32[]{:T(128)} %bitcast.54, f32[]{:T(128)} %bitcast.53, f32[]{:T(128)} %bitcast.52, f32[]{:T(128)} %bitcast.51, f32[]{:T(128)} %bitcast.50, f32[]{:T(128)} %bitcast.49, f32[]{:T(128)} %bitcast.48, f32[]{:T(128)} %bitcast.47, ...), kind=kLoop, calls=%fused_computation.50 | loop fusion | flops 35651584 | bytes 75497512 | tf_op jit(solution)/shard_map/div | solution.py:28
  268.6 9.2 reshape.1955
  277.8 31.8 %add_divide_fusion.7 = f32[1,8,128,16,128]{4,3,2,1,0:T(8,128)} fusion(f32[]{:T(128)} %bitcast.66, f32[]{:T(128)} %bitcast.65, f32[]{:T(128)} %bitcast.64, f32[]{:T(128)} %bitcast.63, f32[]{:T(128)} %bitcast.62, f32[]{:T(128)} %bitcast.61, f32[]{:T(128)} %bitcast.60, f32[]{:T(128)} %bitcast.59, f32[]{:T(128)} %bitcast.58, f32[]{:T(128)} %bitcast.57, ...), kind=kLoop, calls=%fused_computation.49 | loop fusion | flops 35651584 | bytes 75497512 | tf_op jit(solution)/shard_map/div | solution.py:28
  309.6 9.7 reshape.1957
  319.4 31.7 %add_divide_fusion.6 = f32[1,8,128,16,128]{4,3,2,1,0:T(8,128)} fusion(f32[]{:T(128)} %bitcast.76, f32[]{:T(128)} %bitcast.75, f32[]{:T(128)} %bitcast.74, f32[]{:T(128)} %bitcast.73, f32[]{:T(128)} %bitcast.72, f32[]{:T(128)} %bitcast.71, f32[]{:T(128)} %bitcast.70, f32[]{:T(128)} %bitcast.69, f32[]{:T(128)} %bitcast.68, f32[]{:T(128)} %bitcast.67, ...), kind=kLoop, calls=%fused_computation.48 | loop fusion | flops 35651584 | bytes 75497512 | tf_op jit(solution)/shard_map/div | solution.py:28
  351.1 9.2 reshape.1959
  360.3 31.9 %add_divide_fusion.5 = f32[1,8,128,16,128]{4,3,2,1,0:T(8,128)} fusion(f32[]{:T(128)} %bitcast.86, f32[]{:T(128)} %bitcast.85, f32[]{:T(128)} %bitcast.84, f32[]{:T(128)} %bitcast.83, f32[]{:T(128)} %bitcast.82, f32[]{:T(128)} %bitcast.81, f32[]{:T(128)} %bitcast.80, f32[]{:T(128)} %bitcast.79, f32[]{:T(128)} %bitcast.78, f32[]{:T(128)} %bitcast.77, ...), kind=kLoop, calls=%fused_computation.47 | loop fusion | flops 35651584 | bytes 75497512 | tf_op jit(solution)/shard_map/div | solution.py:28
  392.3 9.2 reshape.1961
  401.5 31.8 %add_divide_fusion.4 = f32[1,8,128,16,128]{4,3,2,1,0:T(8,128)} fusion(f32[]{:T(128)} %bitcast.96, f32[]{:T(128)} %bitcast.95, f32[]{:T(128)} %bitcast.94, f32[]{:T(128)} %bitcast.93, f32[]{:T(128)} %bitcast.92, f32[]{:T(128)} %bitcast.91, f32[]{:T(128)} %bitcast.90, f32[]{:T(128)} %bitcast.89, f32[]{:T(128)} %bitcast.88, f32[]{:T(128)} %bitcast.87, ...), kind=kLoop, calls=%fused_computation.46 | loop fusion | flops 35651584 | bytes 75497512 | tf_op jit(solution)/shard_map/div | solution.py:28
  433.3 9.3 reshape.1963
  442.5 31.7 %add_divide_fusion.3 = f32[1,8,128,16,128]{4,3,2,1,0:T(8,128)} fusion(f32[]{:T(128)} %bitcast.106, f32[]{:T(128)} %bitcast.105, f32[]{:T(128)} %bitcast.104, f32[]{:T(128)} %bitcast.103, f32[]{:T(128)} %bitcast.102, f32[]{:T(128)} %bitcast.101, f32[]{:T(128)} %bitcast.100, f32[]{:T(128)} %bitcast.99, f32[]{:T(128)} %bitcast.98, f32[]{:T(128)} %bitcast.97, ...), kind=kLoop, calls=%fused_computation.45 | loop fusion | flops 35651584 | bytes 75497512 | tf_op jit(solution)/shard_map/div | solution.py:28
  474.2 9.2 reshape.1965
  483.5 31.6 %add_divide_fusion.2 = f32[1,8,128,16,128]{4,3,2,1,0:T(8,128)} fusion(f32[]{:T(128)} %bitcast.116, f32[]{:T(128)} %bitcast.115, f32[]{:T(128)} %bitcast.114, f32[]{:T(128)} %bitcast.113, f32[]{:T(128)} %bitcast.112, f32[]{:T(128)} %bitcast.111, f32[]{:T(128)} %bitcast.110, f32[]{:T(128)} %bitcast.109, f32[]{:T(128)} %bitcast.108, f32[]{:T(128)} %bitcast.107, ...), kind=kLoop, calls=%fused_computation.44 | loop fusion | flops 35651584 | bytes 75497512 | tf_op jit(solution)/shard_map/div | solution.py:28
  515.1 9.3 reshape.1967
  524.3 31.7 %add_divide_fusion.1 = f32[1,8,128,16,128]{4,3,2,1,0:T(8,128)} fusion(f32[]{:T(128)} %bitcast.126, f32[]{:T(128)} %bitcast.125, f32[]{:T(128)} %bitcast.124, f32[]{:T(128)} %bitcast.123, f32[]{:T(128)} %bitcast.122, f32[]{:T(128)} %bitcast.121, f32[]{:T(128)} %bitcast.120, f32[]{:T(128)} %bitcast.119, f32[]{:T(128)} %bitcast.118, f32[]{:T(128)} %bitcast.117, ...), kind=kLoop, calls=%fused_computation.43 | loop fusion | flops 35651584 | bytes 75497512 | tf_op jit(solution)/shard_map/div | solution.py:28
  556.0 9.3 reshape.1969
  565.3 32.0 %add_divide_fusion = f32[1,8,128,16,128]{4,3,2,1,0:T(8,128)} fusion(f32[]{:T(128)} %bitcast.136, f32[]{:T(128)} %bitcast.135, f32[]{:T(128)} %bitcast.134, f32[]{:T(128)} %bitcast.133, f32[]{:T(128)} %bitcast.132, f32[]{:T(128)} %bitcast.131, f32[]{:T(128)} %bitcast.130, f32[]{:T(128)} %bitcast.129, f32[]{:T(128)} %bitcast.128, f32[]{:T(128)} %bitcast.127, ...), kind=kLoop, calls=%fused_computation.42 | loop fusion | flops 35651584 | bytes 75497512 | tf_op jit(solution)/shard_map/div | solution.py:28
  597.4 9.3 reshape.1971
  609.1 7.8 constant_dynamic-update-slice_fusion.10
  616.9 7.9 constant_dynamic-update-slice_fusion.9
  633.1 7.8 constant_dynamic-update-slice_fusion.6
  649.3 7.8 constant_dynamic-update-slice_fusion.3
  665.1 7.8 constant_dynamic-update-slice_fusion
  672.9 79.0 %select_reduce_fusion = (f32[1024,2048]{1,0:T(8,128)}, f32[1024,2048]{1,0:T(8,128)}, f32[1024,2048]{1,0:T(8,128)}, f32[1024,2048]{1,0:T(8,128)}) fusion(f32[12,1024,2048]{2,1,0:T(8,128)} %constant_dynamic-update-slice_fusion, pred[12]{0:T(512)(128)(4,1)S(1)} %copy-done.8, pred[12]{0:T(512)(128)(4,1)S(1)} %copy-done.9, pred[12]{0:T(512)(128)(4,1)S(1)} %copy-done.7, ...), kind=kLoop, calls=%fused_computation.31 | loop fusion | flops 192937984 | bytes 134217776 | tf_op jit(solution)/shard_map/reduce_max | solution.py:33
  751.9 94.0 %exponential_reduce_fusion.1 = (f32[1024,2048]{1,0:T(8,128)}, f32[1024,2048]{1,0:T(8,128)}, f32[1024,2048]{1,0:T(8,128)}, f32[1024,2048]{1,0:T(8,128)}) fusion(f32[12,1024,2048]{2,1,0:T(8,128)} %constant_dynamic-update-slice_fusion, f32[1024,2048]{1,0:T(8,128)} %get-tuple-element.125, pred[12]{0:T(512)(128)(4,1)S(1)} %copy-done.8, ...), kind=kLoop, calls=%fused_computation.30 | loop fusion | flops 293601280 | bytes 167772208 | tf_op jit(solution)/shard_map/reduce_sum | solution.py:38
  845.9 38.0 %fusion.16 = (f32[1,1024,2048]{2,1,0:T(8,128)}, f32[1024,2048]{1,0:T(8,128)}, f32[1,1024,2048]{2,1,0:T(8,128)}, f32[1,1024,2048]{2,1,0:T(8,128)}, f32[1,1024,2048]{2,1,0:T(8,128)}) fusion(f32[1024,2048]{1,0:T(8,128)} %get-tuple-element.128, f32[1024,2048]{1,0:T(8,128)} %get-tuple-element.124, f32[]{:T(128)} %bitcast.16, f32[1024,2048]{1,0:T(8,128)} %get-tuple-element.125, ...), kind=kLoop, calls=%fused_computation.62 | loop fusion | flops 23068672 | bytes 109051920 | tf_op jit(solution)/shard_map/mul | solution.py:39
  886.1 5.4 all-to-all-start.2
  893.9 7.7 all-to-all-start.1
  901.6 18.8 %fusion.13 = f32[1024,2048]{1,0:T(8,128)} fusion(f32[1,1024,2048]{2,1,0:T(8,128)} %get-tuple-element.181, f32[1,1024,2048]{2,1,0:T(8,128)} %get-tuple-element.180, f32[1,1024,2048]{2,1,0:T(8,128)} %get-tuple-element.179, f32[1,1024,2048]{2,1,0:T(8,128)} %get-tuple-element.177, f32[1024,2048]{1,0:T(8,128)} %get-tuple-element.178), kind=kLoop, calls=%fused_computation.40 | loop fusion | flops 39845888 | bytes 50331648 | tf_op jit(solution)/shard_map/reduce_sum | solution.py:42
  920.4 12.0 %log_add_fusion = f32[1024,2048]{1,0:T(8,128)} fusion(f32[1024,2048]{1,0:T(8,128)} %get-tuple-element.178, f32[1024,2048]{1,0:T(8,128)} %fusion.13), kind=kLoop, calls=%fused_computation.54 | loop fusion | flops 2097152 | bytes 25165824 | tf_op jit(solution)/shard_map/add | solution.py:42
  935.9 5.8 gather_fusion.1
  941.8 5.9 all-to-all-done.1
  947.7 41.6 %while.33 = (s32[]{:T(128)}, bf16[16,16,32]{2,1,0:T(8,128)(2,1)S(1)}, f32[]{:T(128)}, f32[16,16,2048]{2,1,0:T(8,128)S(1)}, bf16[16,16,32,128]{3,2,1,0:T(8,128)(2,1)}, /*index=5*/bf16[128,2048]{1,0:T(8,128)(2,1)}) while((s32[]{:T(128)}, bf16[16,16,32]{2,1,0:T(8,128)(2,1)S(1)}, f32[]{:T(128)}, f32[16,16,2048]{2,1,0:T(8,128)S(1)}, ...), condition=%wide.region_16.17_spmd.clone, body=%wide.region_14.16_spmd.sunk.clone | while | flops 270564864 | bytes 1058385 | solution.py:68
  989.3 11.0 pmax.7
  1000.4 54.8 %while.34 = (s32[]{:T(128)}, f32[16,16,32]{2,1,0:T(8,128)}, f32[]{:T(128)}, f32[16,16,2048]{2,1,0:T(8,128)S(1)}, bf16[16,16,32,128]{3,2,1,0:T(8,128)(2,1)}, /*in...) while((s32[]{:T(128)}, f32[16,16,32]{2,1,0:T(8,128)}, f32[]{:T(128)}, ...), condition=%wide.region_20.21_spmd.clone, body=%wide.region_18.20_spmd.sunk.clone | while | flops 271613440 | bytes 1068121 | solution.py:75
  1055.2 13.3 %psum.7 = f32[16,16,32]{2,1,0:T(8,128)} all-reduce(f32[16,16,32]{2,1,0:T(8,128)} %get-tuple-element.119), channel_id=1, replica_groups=mesh['orig'=8,'dest'=4] {'dest'}, use_global_device_ids=true, to_apply=%region_21.22 | all-reduce | flops 8192 | bytes 65536 | tf_op jit(solution)/shard_map/psum | solution.py:76
  1068.5 73.9 %while.35 = (s32[]{:T(128)}, f32[16,16,2048]{2,1,0:T(8,128)}, f32[]{:T(128)}, f32[16,16,2048]{2,1,0:T(8,128)S(1)}, bf16[16,16,32,128]{3,2,1,0:T(8,128)(2,1)}, /*...) while((s32[]{:T(128)}, f32[16,16,2048]{2,1,0:T(8,128)}, ...), condition=%wide.region_24.25_spmd.clone, body=%wide.region_22.24_spmd.sunk.clone | while | flops 273678336 | bytes 1461357 | solution.py:83
  1144.2 7.6 scatter_custom_fusion
  (294 shorter events, 229.7 us)
Async XLA Ops:
  0.6 606.1 %copy-start = (bf16[4096,128]{1,0:T(8,128)(2,1)S(1)}, bf16[4096,128]{1,0:T(8,128)(2,1)}, u32[]{:S(2)}) copy-start(bf16[4096,128]{1,0:T(8,128)(2,1)} %param.24) | copy-start | bytes 3145732
  2.1 22.3 %copy-start.4 = (s32[1024]{0:T(1024)}, s32[1024]{0:T(1024)S(1)}, u32[]{:S(2)}) copy-start(s32[1024]{0:T(1024)S(1)} %pad_clamp_fusion.1) | copy-start | bytes 12292
  7.2 878.9 %all-to-all-start = ((s32[8,1,32]{2,1,0:T(1,128)}), s32[8,1,32]{2,1,0:T(1,128)}, u32[]{:S(2)}, u32[]{:S(2)}) async-start(s32[8,1,32]{2,1,0:T(1,128)} %select_n.102), calls=%async_computation | async-start | bytes 8192 | tf_op jit(solution)/shard_map/all_to_all | solution.py:126
  28.5 33.2 %copy-start.2 = (f32[12]{0:T(128)S(1)}, f32[12]{0:T(128)}, u32[]{:S(2)}) copy-start(f32[12]{0:T(128)} %param.20) | copy-start | bytes 148
  28.5 33.9 %copy-start.3 = (f32[8,8,16]{2,1,0:T(8,128)S(1)}, f32[8,8,16]{2,1,0:T(8,128)}, u32[]{:S(2)}) copy-start(f32[8,8,16]{2,1,0:T(8,128)} %param.18) | copy-start | bytes 12292
  609.0 15.7 %slice-start = ((s8[8388608]{0:T(1024)(128)(4,1)}), s8[4194304]{0:T(1024)(128)(4,1)S(1)}, s32[]{:S(2)}) async-start(s8[8388608]{0:T(1024)(128)(4,1)} %bitcast.256), calls=%async_computation.3 | async-start | bytes 8388608
  616.9 7.9 slice-start.1
  616.9 12.0 %slice-start.2 = ((s8[8388608]{0:T(1024)(128)(4,1)}), s8[4194304]{0:T(1024)(128)(4,1)S(1)}, s32[]{:S(2)}) async-start(s8[8388608]{0:T(1024)(128)(4,1)} %bitcast.258), calls=%async_computation.5 | async-start | bytes 8388608
  624.8 4.2 slice-start.3
  628.9 12.0 %slice-start.4 = ((s8[8388608]{0:T(1024)(128)(4,1)}), s8[4194304]{0:T(1024)(128)(4,1)S(1)}, s32[]{:S(2)}) async-start(s8[8388608]{0:T(1024)(128)(4,1)} %bitcast.260), calls=%async_computation.7 | async-start | bytes 8388608
  633.1 7.8 slice-start.5
  633.1 12.0 %slice-start.6 = ((s8[8388608]{0:T(1024)(128)(4,1)}), s8[4194304]{0:T(1024)(128)(4,1)S(1)}, s32[]{:S(2)}) async-start(s8[8388608]{0:T(1024)(128)(4,1)} %bitcast.262), calls=%async_computation.9 | async-start | bytes 8388608
  641.0 4.2 slice-start.7
  645.1 12.0 %slice-start.8 = ((s8[8388608]{0:T(1024)(128)(4,1)}), s8[4194304]{0:T(1024)(128)(4,1)S(1)}, s32[]{:S(2)}) async-start(s8[8388608]{0:T(1024)(128)(4,1)} %bitcast.264), calls=%async_computation.11 | async-start | bytes 8388608
  649.3 7.8 slice-start.9
  649.3 12.0 %slice-start.10 = ((s8[8388608]{0:T(1024)(128)(4,1)}), s8[4194304]{0:T(1024)(128)(4,1)S(1)}, s32[]{:S(2)}) async-start(s8[8388608]{0:T(1024)(128)(4,1)} %bitcast.266), calls=%async_computation.13 | async-start | bytes 8388608
  657.1 4.2 slice-start.11
  665.1 7.8 copy-start.6
  665.1 7.8 copy-start.7
  665.1 7.8 copy-start.8
  665.1 7.8 copy-start.9
  845.9 38.0 %copy-start.1 = (bf16[256,32,128]{2,1,0:T(8,128)(2,1)S(1)}, bf16[256,32,128]{2,1,0:T(8,128)(2,1)}, u32[]{:S(2)}) copy-start(bf16[256,32,128]{2,1,0:T(8,128)(2,1)} %gather_fusion.2) | copy-start | bytes 6291460
  845.9 38.0 %copy-start.10 = (pred[8,32]{1,0:T(8,128)(4,1)S(1)}, pred[8,32]{1,0:T(8,128)(4,1)}, u32[]{:S(2)}) copy-start(pred[8,32]{1,0:T(8,128)(4,1)} %broadcast_in_dim.136) | copy-start | bytes 772
  845.9 39.6 %copy-start.5 = (s32[256]{0:T(256)S(1)}, s32[256]{0:T(256)}, u32[]{:S(2)}) copy-start(s32[256]{0:T(256)} %get-tuple-element.277) | copy-start | bytes 3076
  886.1 7.8 all-to-all-start.2
  893.9 53.8 %all-to-all-start.1 = ((bf16[8,32,32,128]{3,2,1,0:T(8,128)(2,1)}), bf16[8,32,32,128]{3,2,1,0:T(8,128)(2,1)}, u32[]{:S(2)}, u32[]{:S(2)}) async-start(bf16[8,32,32,128]{3,2,1,0:T(8,128)(2,1)} %broadcast_select_fusion), calls=%async_computation.1 | async-start | bytes 4194304 | tf_op jit(solution)/shard_map/all_to_all | solution.py:125
where the time goes:
time: 1170 us; the launch traced here: 1150 us
  other arithmetic  716 us (61%)
  local copies, waits for them, and re-layouts  277 us (24%)
  matrix products  106 us (9%)
  blocking collectives  24.4 us (2%)
  starting transfers between devices  18.6 us (2%)
    div x12, other arithmetic, nest_logsum(): utils.append(value / mode_theta[mode_index])  381 us
    div x12, local copies, waits for them, and re-layouts, nest_logsum(): utils.append(value / mode_theta[mode_index])  112 us
    dot_general x48, matrix products, group_scores(): jnp.dot(feat_part.reshape(block_num * tour_size, features), zone_attr, pr...  106 us
    unnamed x58, local copies, waits for them, and re-layouts  96.2 us
    reduce_sum x1, other arithmetic, nest_logsum(): sum_total = jnp.sum(jnp.exp(shifted), axis=0)  94 us
    reduce_max x1, other arithmetic, nest_logsum(): maxima.append(jnp.max(jnp.where(member, scaled_util, neg_fill), axis=0))  79 us
    mul x1, other arithmetic, nest_logsum(): scaled * scale_part[:, :, None, :, None]  44.3 us
    mul x1, other arithmetic, nest_logsum(): nest_theta[nest_index] * (maxima[nest_index] + jnp.log(sum_total))  38 us
  transfers between devices with their start and end apart: 3, of which 2 were waited for; matrix products, arithmetic and copies ran while one was open for 79% of the time, Pallas kernels for 0%

commit v1 on v0

v1 whole, which is shorter than its diff:
```python
import functools
import math

import jax
import jax.numpy as jnp
from jax import lax
from jax.experimental import pallas as pl
from jax.experimental.pallas import tpu as pltpu
from jax.sharding import PartitionSpec as P

LOG2E = math.log2(math.e)
LN2 = math.log(2.0)
ROWS = 16


def split_pieces(value, count):
    pieces = []
    rest = value
    for _ in range(count):
        piece = lax.reduce_precision(rest, 8, 7)
        pieces.append(piece)
        rest = rest - piece
    return pieces


def logsum_kernel(
    keep_ref, inv_ref, theta_ref, end_ref, skim_ref, weight_ref, out_ref, w_scratch, *acc_refs
):
    tables, block_rows, width = skim_ref.shape
    modes = weight_ref.shape[3]
    depth = tables * ROWS
    nests = theta_ref.shape[0]
    row_id = lax.broadcasted_iota(jnp.int32, (ROWS, depth), 0)
    lane_id = lax.broadcasted_iota(jnp.int32, (ROWS, depth), 1)
    diagonal = lax.rem(lane_id, ROWS) == row_id
    groups = block_rows // ROWS
    pair = len(acc_refs)

    def column_block(index, carry):
        cols = pl.ds(pl.multiple_of(index * 128, 128), 128)
        for mode in range(modes):
            for piece in range(4):
                row = weight_ref[0, index, piece, pl.ds(mode, 1), :]
                tile = jnp.broadcast_to(row, (ROWS, depth))
                if piece < 3:
                    tile = jnp.where(diagonal, tile, 0.0)
                w_scratch[mode * ROWS:(mode + 1) * ROWS, piece * depth:(piece + 1) * depth] = (
                    tile.astype(jnp.bfloat16)
                )
        ones = jnp.ones((depth, 128 * pair), jnp.bfloat16)
        for start in range(0, groups, pair):
            parts = []
            for group in range(start, start + pair):
                parts.append(
                    skim_ref[:, group * ROWS:(group + 1) * ROWS, cols].reshape(depth, 128)
                )
            data = jnp.concatenate(parts, axis=1)
            stacked = jnp.concatenate([data, data, data, ones], axis=0)
            util = jnp.dot(w_scratch[...], stacked, preferred_element_type=jnp.float32)
            for offset in range(pair):
                acc_ref = acc_refs[offset]
                part = util[:, offset * 128:(offset + 1) * 128].reshape(modes, ROWS, 128)
                top = part[0]
                for mode in range(1, modes):
                    top = jnp.maximum(top, part[mode])
                acc = None
                for mode in range(modes):
                    term = jnp.exp2((part[mode] - top) * inv_ref[mode])
                    acc = term if acc is None else term + keep_ref[mode] * acc
                    acc_ref[mode] = acc
                total = None
                for nest in range(nests):
                    nest_sum = jnp.maximum(acc_ref[end_ref[nest]], 1.2e-38)
                    value = jnp.exp2(theta_ref[nest] * jnp.log2(nest_sum))
                    total = value if total is None else total + value
                group = start + offset
                out_ref[group * ROWS:(group + 1) * ROWS, cols] = (top + jnp.log2(total)) * LN2
        return carry

    lax.fori_loop(0, width // 128, column_block, 0)


def nest_logsum(skim_part, scale_part, mode_coef, mode_const, nest_theta, mode_nest):
    tables, row_count, col_count = skim_part.shape
    block_rows = row_count // scale_part.shape[1]
    block_cols = col_count // scale_part.shape[2]
    nests = nest_theta.shape[0]
    modes = mode_coef.shape[0]
    depth = tables * ROWS
    mode_ids = jnp.arange(modes)
    before = (mode_nest[None, :] < mode_nest[:, None]) | (
        (mode_nest[None, :] == mode_nest[:, None]) & (mode_ids[None, :] < mode_ids[:, None])
    )
    rank = jnp.sum(before.astype(jnp.int32), axis=1)
    place = rank[None, :] == mode_ids[:, None]
    coef = jnp.sum(jnp.where(place[:, :, None], mode_coef[None], 0.0), axis=1) * LOG2E
    const = jnp.sum(jnp.where(place, mode_const[None], 0.0), axis=1) * LOG2E
    nest = jnp.sum(jnp.where(place, mode_nest[None], 0), axis=1)
    inverse = jnp.sum(
        jnp.where(nest[:, None] == jnp.arange(nests)[None, :], 1.0 / nest_theta[None, :], 0.0), axis=1
    )
    keep = jnp.concatenate([jnp.zeros((1,), jnp.float32), (nest[1:] == nest[:-1]).astype(jnp.float32)])
    ends = jnp.sum((mode_nest[None, :] <= jnp.arange(nests)[:, None]).astype(jnp.int32), axis=1) - 1
    weight = jnp.transpose(scale_part, (1, 2, 0))[:, :, None, :] * coef[None, None]
    pieces = [jnp.repeat(piece, ROWS, axis=-1) for piece in split_pieces(weight, 3)]
    lanes = jnp.arange(depth)[None, :]
    const_piece = jnp.zeros((modes, depth), jnp.float32)
    for index, piece in enumerate(split_pieces(const, 3)):
        const_piece = jnp.where(lanes == index, piece[:, None], const_piece)
    pieces.append(jnp.broadcast_to(const_piece, pieces[0].shape))
    weights = jnp.stack(pieces, axis=2)
    width = min(col_count, 1024)
    per = width // block_cols
    pair = 2
    smem = pl.BlockSpec(memory_space=pltpu.SMEM)
    return pl.pallas_call(
        logsum_kernel,
        grid=(row_count // block_rows, col_count // width),
        out_shape=jax.ShapeDtypeStruct((row_count, col_count), jnp.float32),
        in_specs=[
            smem, smem, smem, smem,
            pl.BlockSpec((tables, block_rows, width), lambda i, j: (0, i, j)),
            pl.BlockSpec((1, per, 4, modes, depth), lambda i, j: (i, j, 0, 0, 0)),
        ],
        out_specs=pl.BlockSpec((block_rows, width), lambda i, j: (i, j)),
        scratch_shapes=[pltpu.VMEM((modes * ROWS, 4 * depth), jnp.bfloat16)]
        + [pltpu.VMEM((modes, ROWS, 128), jnp.float32)] * pair,
        compiler_params=pltpu.CompilerParams(vmem_limit_bytes=40 * 1024 * 1024),
        cost_estimate=pl.CostEstimate(
            flops=200 * row_count * col_count,
            bytes_accessed=(2 * tables + 4) * row_count * col_count,
            transcendentals=21 * row_count * col_count,
        ),
        name="logsum",
    )(keep, inverse, nest_theta, ends, skim_part, weights)


def stats_kernel(zone_ref, count_ref, coef_ref, feat_ref, attr_ref, rows_ref, out_ref, score_ref, lse_ref):
    tours = feat_ref.shape[0]
    tour_size = tours // 8
    step = pl.program_id(0)
    factor = coef_ref[0] * LOG2E
    score_ref[...] = jnp.dot(feat_ref[...], attr_ref[...], preferred_element_type=jnp.float32)
    for block in range(8):
        home = rows_ref[pl.ds(zone_ref[step * 8 + block], 1), :] * factor
        for start in range(0, tour_size, ROWS):
            base = block * tour_size + start

            @pl.when(count_ref[step * 8 + block] > start)
            def _():
                score = score_ref[base:base + ROWS, :] * LOG2E + home
                top = jnp.max(score, axis=1, keepdims=True)
                total = jnp.sum(jnp.exp2(score - top), axis=1, keepdims=True)
                lse_ref[base:base + ROWS, :] = jnp.broadcast_to(top + jnp.log2(total), (ROWS, 128))

    for part in range(tours // 128):
        turned = jnp.transpose(lse_ref[part * 128:(part + 1) * 128, :])
        out_ref[0, part:part + 1, :] = turned[0:1, :]


def trips_kernel(
    zone_ref, count_ref, coef_ref, feat_ref, attr_ref, rows_ref, parts_ref, out_ref, score_ref, bias_ref, *, scale
):
    tours = feat_ref.shape[0]
    tour_size = tours // 8
    step = pl.program_id(0)
    width = out_ref.shape[1]
    factor = coef_ref[0] * LOG2E

    @pl.when(step == 0)
    def _():
        out_ref[...] = jnp.zeros_like(out_ref)

    score_ref[...] = jnp.dot(feat_ref[...], attr_ref[...], preferred_element_type=jnp.float32)
    parts = parts_ref[:, 0]
    top = jnp.max(parts, axis=0)
    lse = top + jnp.log2(jnp.sum(jnp.exp2(parts - top[None]), axis=0))
    for part in range(tours // 128):
        bias_ref[part * 128:(part + 1) * 128, :] = jnp.transpose(
            jnp.broadcast_to(lse[part:part + 1, :], (128, 128))
        )
    row_id = lax.broadcasted_iota(jnp.int32, (ROWS, 128), 0)
    for block in range(8):
        zone = zone_ref[step * 8 + block]
        count = count_ref[step * 8 + block]
        home = rows_ref[pl.ds(zone, 1), :] * factor
        for start in range(0, tour_size, ROWS):
            base = block * tour_size + start

            @pl.when(count > start)
            def _():
                bias = jnp.where(row_id < count - start, bias_ref[base:base + ROWS, :], 1e30)
                wide = jnp.concatenate([bias] * (width // 128), axis=1)
                score = score_ref[base:base + ROWS, :] * LOG2E + home
                total = jnp.sum(jnp.exp2(score - wide), axis=0, keepdims=True)
                out_ref[pl.ds(zone, 1), :] = out_ref[pl.ds(zone, 1), :] + scale * total


def tour_trips(feats, logsums, zones, counts, zone_attr, logsum_coef, scale):
    tours, features = feats.shape
    slots = zones.shape[0]
    anchors, width = logsums.shape
    steps = slots // 8
    group = tours // steps
    smem = pl.BlockSpec(memory_space=pltpu.SMEM)
    once = pl.Buffered(1)
    common = [
        smem, smem, smem,
        pl.BlockSpec((group, features), lambda i: (i, 0)),
        pl.BlockSpec((features, width), lambda i: (0, 0), pipeline_mode=once),
        pl.BlockSpec((anchors, width), lambda i: (0, 0), pipeline_mode=once),
    ]
    params = pltpu.CompilerParams(vmem_limit_bytes=48 * 1024 * 1024)
    lines = group // 128
    local_lse = pl.pallas_call(
        stats_kernel,
        grid=(steps,),
        out_shape=jax.ShapeDtypeStruct((steps, lines, 128), jnp.float32),
        in_specs=common,
        out_specs=pl.BlockSpec((1, lines, 128), lambda i: (i, 0, 0)),
        scratch_shapes=[pltpu.VMEM((group, width), jnp.float32), pltpu.VMEM((group, 128), jnp.float32)],
        compiler_params=params,
        name="stats",
    )(zones, counts, logsum_coef, feats, zone_attr, logsums)
    gathered = lax.all_gather(local_lse, "dest")
    return pl.pallas_call(
        functools.partial(trips_kernel, scale=scale),
        grid=(steps,),
        out_shape=jax.ShapeDtypeStruct((anchors, width), jnp.float32),
        in_specs=common
        + [pl.BlockSpec((gathered.shape[0], 1, lines, 128), lambda i: (0, i, 0, 0))],
        out_specs=pl.BlockSpec((anchors, width), lambda i: (0, 0), pipeline_mode=once),
        scratch_shapes=[pltpu.VMEM((group, width), jnp.float32), pltpu.VMEM((group, 128), jnp.float32)],
        compiler_params=params,
        name="trips",
    )(zones, counts, logsum_coef, feats, zone_attr, logsums, gathered)


def local(
    skim_tables,
    block_scale,
    mode_coef,
    mode_const,
    nest_theta,
    mode_nest,
    logsum_coef,
    tour_attr,
    zone_attr,
    block_zone,
    block_count,
):
    sources = lax.axis_size("orig")
    blocks_here = block_zone.shape[0]
    anchors = skim_tables.shape[1]
    tour_size = tour_attr.shape[0] // blocks_here
    features = tour_attr.shape[1]
    capacity = max(2, 2 * blocks_here // sources)
    slot_count = sources * capacity
    factor = anchors * sources / tour_size
    source_dev = block_zone // anchors
    local_zone = block_zone - source_dev * anchors
    block_ids = jnp.arange(blocks_here)
    same = (source_dev[:, None] == source_dev[None, :]) & (block_ids[None, :] < block_ids[:, None])
    slot_rank = jnp.sum(same.astype(jnp.int32), axis=1)
    slot_of_block = source_dev * capacity + slot_rank
    slot_match = slot_of_block[None, :] == jnp.arange(slot_count)[:, None]
    code = local_zone * 64 + block_count
    send_code = jnp.sum(jnp.where(slot_match, code[None, :], 0), axis=1)
    tour_feats = tour_attr.reshape(blocks_here, tour_size * features)
    send_feats = jnp.dot(slot_match.astype(jnp.bfloat16), tour_feats)
    recv_feats = lax.all_to_all(
        send_feats.reshape(sources, capacity * tour_size, features), "orig", split_axis=0, concat_axis=0, tiled=True
    )
    recv_code = lax.all_to_all(
        send_code.reshape(sources, capacity), "orig", split_axis=0, concat_axis=0, tiled=True
    ).reshape(slot_count)
    logsums = nest_logsum(skim_tables, block_scale, mode_coef, mode_const, nest_theta, mode_nest)
    trip_matrix = tour_trips(
        recv_feats.reshape(slot_count * tour_size, features),
        logsums,
        recv_code // 64,
        recv_code % 64,
        zone_attr,
        logsum_coef,
        factor,
    )
    return (logsums, trip_matrix)


def solution(mesh):
    return jax.shard_map(
        local,
        mesh=mesh,
        in_specs=(
            P(None, "orig", "dest"),
            P(None, "orig", "dest"),
            P(),
            P(),
            P(),
            P(),
            P(),
            P("orig", None),
            P(None, "dest"),
            P("orig"),
            P("orig"),
        ),
        out_specs=(P("orig", "dest"), P("orig", "dest")),
        check_vma=False,
    )
```

time: 1170 us -> 280 us (0.24); the launches traced: 1150 us -> 280 us
  other arithmetic: 716 us -> 5.73 us
  local copies, waits for them, and re-layouts: 277 us -> 39.8 us
  Pallas kernels: 0 us -> 215 us
  matrix products: 106 us -> 0.7 us
  blocking collectives: 24.4 us -> 7.05 us
    div x12 -> x1, other arithmetic: 381 us -> 0.01 us  [nest_logsum(): 1.0 / nest_theta[None, :]]
    pallas_call x0 -> x3, Pallas kernels: none -> 215 us  [the longest x1 97.1 us: tour_trips(): pl.pallas_call(stats_kernel, grid=(steps,), out_shape=jax.ShapeDtypeStruc...]
    mul x51 -> x1, other arithmetic: 116 us -> 0.01 us  [nest_logsum(): jnp.sum(jnp.where(place[:, :, None], mode_coef[None], 0.0), axis=1) * LOG2E]
    reduce_sum x5 -> x8, other arithmetic: 114 us -> 0.99 us  [the longest x1 0.18 us: nest_logsum(): rank = jnp.sum(before.astype(jnp.int32), axis=1)]
    div x12 -> x0, local copies, waits for them, and re-layouts: 112 us -> none  [nest_logsum(): utils.append(value / mode_theta[mode_index])]
    dot_general x48 -> x1, matrix products: 106 us -> 0.7 us  [local(): send_feats = jnp.dot(slot_match.astype(jnp.bfloat16), tour_feats)]
    unnamed x58 -> x12, local copies, waits for them, and re-layouts: 96.2 us -> 0.03 us
    reduce_max x1 -> x0, other arithmetic: 79 us -> none  [nest_logsum(): maxima.append(jnp.max(jnp.where(member, scaled_util, neg_fill), axis=0))]
  transfers between devices with their start and end apart: 3 -> 2, of which waited for: 2 -> 0; matrix products, arithmetic and copies ran while one was open for 79% -> 16% of each run, Pallas kernels for 0% -> 26%
where the time goes in v1:
time: 280 us
  Pallas kernels  215 us (77%)
  local copies, waits for them, and re-layouts  39.8 us (14%)
  starting transfers between devices  10.9 us (4%)
  blocking collectives  7.05 us (3%)
  other arithmetic  5.73 us (2%)
    pallas_call x1, Pallas kernels, tour_trips(): pl.pallas_call(stats_kernel, grid=(steps,), out_shape=jax.ShapeDtypeStruc...  97.1 us
    pallas_call x1, Pallas kernels, nest_logsum(): pl.pallas_call(logsum_kernel, grid=(row_count // block_rows, col_count //...  74.1 us
    pallas_call x1, Pallas kernels, tour_trips(): pl.pallas_call(functools.partial(trips_kernel, scale=scale), grid=(steps,...  43.5 us
    another operation x7, local copies, waits for them, and re-layouts, nest_logsum(): weights = jnp.stack(pieces, axis=2)  20.6 us
    broadcast_in_dim x3, local copies, waits for them, and re-layouts, nest_logsum(): jnp.repeat(piece, ROWS, axis=-1)  13.9 us
    all_gather x1, blocking collectives, tour_trips(): gathered = lax.all_gather(local_lse, 'dest')  7.05 us
  transfers between devices with their start and end apart: 2, of which 0 were waited for; matrix products, arithmetic and copies ran while one was open for 16% of the time, Pallas kernels for 26%

profile of v1, /device:TPU:25, one launch (start us, length us, event | category | flops | bytes accessed | tf_op | source)
XLA Modules:
  0.0 280.3 jit_solution(13425252801597634142)
XLA Ops:
  0.6 0.7 multiply_add_fusion
  1.3 0.2 convert_reduce_fusion
  1.5 0.1 select_reduce_fusion
  1.6 0.7 all_to_all.9
  2.3 5.5 %all-to-all-start = ((s32[8,1,32]{2,1,0:T(1,128)}), s32[8,1,32]{2,1,0:T(1,128)S(1)}, u32[]{:S(2)}, u32[]{:S(2)}) async-start(s32[8,1,32]{2,1,0:T(1,128)} %all_to_all.9), calls=%async_computation | async-start | bytes 8192 | tf_op jit(solution)/shard_map/all_to_all | solution.py:274
  7.8 1.5 reshape.81
  9.3 0.7 fusion.1
  10.0 0.0 copy-start.2
  10.0 0.0 copy-start.4
  10.1 0.0 copy-start.3
  10.1 2.4 reshape.82
  12.4 0.0 all-to-all-done
  12.4 5.4 %all-to-all-start.1 = ((bf16[8,1024,128]{2,1,0:T(8,128)(2,1)}), bf16[8,1024,128]{2,1,0:T(8,128)(2,1)S(1)}, u32[]{:S(2)}, u32[]{:S(2)}) async-start(bf16[8,1024,128]{2,1,0:T(8,128)(2,1)} %reshape.82), calls=%async_computation.1 | async-start | bytes 4194304 | tf_op jit(solution)/shard_map/all_to_all | solution.py:271
  18.5 0.0 copy-done.2
  18.5 0.1 copy.25
  18.6 0.0 copy-done.4
  18.6 0.2 convert_reduce_fusion.1
  18.8 0.0 copy-done.3
  18.8 0.1 select_reduce_fusion.1
  18.9 1.5 multiply_reduce-precision_fusion
  20.4 3.7 %broadcast_in_dim.150 = f32[8,16,12,8,16]{4,3,1,2,0:T(8,128)} broadcast(f32[8,16,12,8]{3,1,2,0:T(8,128)S(1)} %get-tuple-element.4), dimensions={0,1,2,3} | broadcast | bytes 835584 | tf_op jit(solution)/shard_map/broadcast_in_dim | solution.py:105
  24.2 5.1 %stack_reshape.9 = f32[8,16,1,12,128]{4,1,3,0,2:T(8,128)} reshape(f32[8,16,12,8,16]{4,3,1,2,0:T(8,128)} %broadcast_in_dim.150) | data formatting | bytes 1572864 | tf_op jit(solution)/shard_map/stack;reshape | solution.py:111
  29.3 1.4 copy.26
  30.6 5.1 %broadcast_in_dim.151 = f32[8,16,12,8,16]{4,3,1,2,0:T(8,128)} broadcast(f32[8,16,12,8]{3,1,2,0:T(8,128)} %get-tuple-element.5), dimensions={0,1,2,3} | broadcast | bytes 835584 | tf_op jit(solution)/shard_map/broadcast_in_dim | solution.py:105
  35.7 5.1 %stack_reshape.10 = f32[8,16,1,12,128]{4,1,3,0,2:T(8,128)} reshape(f32[8,16,12,8,16]{4,3,1,2,0:T(8,128)} %broadcast_in_dim.151) | data formatting | bytes 1572864 | tf_op jit(solution)/shard_map/stack;reshape | solution.py:111
  40.8 2.4 copy.27
  43.2 5.1 %broadcast_in_dim.152 = f32[8,16,12,8,16]{4,3,1,2,0:T(8,128)} broadcast(f32[8,16,12,8]{3,1,2,0:T(8,128)} %get-tuple-element.6), dimensions={0,1,2,3} | broadcast | bytes 835584 | tf_op jit(solution)/shard_map/broadcast_in_dim | solution.py:105
  48.3 5.1 %stack_reshape.11 = f32[8,16,1,12,128]{4,1,3,0,2:T(8,128)} reshape(f32[8,16,12,8,16]{4,3,1,2,0:T(8,128)} %broadcast_in_dim.152) | data formatting | bytes 1572864 | tf_op jit(solution)/shard_map/stack;reshape | solution.py:111
  53.4 1.4 copy.28
  54.8 0.1 select_reduce_fusion.3
  54.9 0.1 slice_compare_fusion
  55.0 0.1 add_convert_fusion.keep_ref
  55.1 0.1 convert_reduce_fusion.2
  55.2 0.0 copy-done.5
  55.2 0.1 select_reduce_fusion.2
  55.4 0.1 select_reduce_fusion.4.inv_ref
  55.5 0.1 select_select_fusion
  55.5 0.1 stack_broadcast_in_dim.3
  55.6 1.6 pad_maximum_fusion.weight_ref
  57.3 0.0 copy-start
  57.3 74.1 %logsum.1.rows_ref = f32[1024,2048]{1,0:T(8,128)} custom-call(f32[12]{0:T(128)S(1)} %add_convert_fusion.keep_ref, f32[12]{0:T(128)S(1)} %select_reduce_fusion.4.inv_ref, f32[4]{0:T(128)S(1)} %copy-done.1, s32[4]{0:T(128)S(1)} %broadcast_add_fusion.end_ref, bf16[8,1024,2048]{2,1,0:T(8,128)(2,1)} %skim_ref.1, f32[8,16,4,12,128]{4,3,2,1,0:T(8,128)S(1)} %pad_maximum_fusion.weight_ref), custom_call_target="tpu_custom_call" | custom-call | flops 419430400 | bytes 41943040 | tf_op jit(solution)/shard_map/logsum/pallas_call | solution.py:116
  131.4 0.5 broadcast.124
  131.9 0.7 reduce.3
  132.6 0.1 reshape.80
  132.7 0.0 all-to-all-done.1
  132.7 97.1 %stats.1 = f32[32,2,128]{2,1,0:T(2,128)S(1)} custom-call(s32[256]{0:T(256)S(1)} %get-tuple-element.8.zone_ref, s32[256]{0:T(256)S(1)} %get-tuple-element.7.count_ref, f32[1]{0:T(128)S(6)} %copy.29.coef_ref, bf16[8192,128]{1,0:T(8,128)(2,1)S(1)} %bitcast.16, bf16[128,2048]{1,0:T(8,128)(2,1)S(1)} %copy-done, f32[1024,2048]{1,0:T(8,128)} %logsum.1.rows_ref), custom_call_target="tpu_custom_call" | custom-call | tf_op jit(solution)/shard_map/stats/pallas_call | solution.py:215
  229.8 7.1 %all-gather = f32[128,2,128]{2,1,0:T(2,128)S(1)} all-gather(f32[32,2,128]{2,1,0:T(2,128)S(1)} %stats.1), channel_id=2, replica_groups=mesh['orig'=8,'dest'=4] {'dest'}, dimensions={0}, use_global_device_ids=true | all-gather | bytes 163840 | tf_op jit(solution)/shard_map/all_gather | solution.py:225
  236.9 43.5 %trips.1 = f32[1024,2048]{1,0:T(8,128)} custom-call(s32[256]{0:T(256)S(1)} %get-tuple-element.8.zone_ref, s32[256]{0:T(256)S(1)} %get-tuple-element.7.count_ref, f32[1]{0:T(128)S(6)} %copy.29.coef_ref, bf16[8192,128]{1,0:T(8,128)(2,1)S(1)} %bitcast.17, bf16[128,2048]{1,0:T(8,128)(2,1)S(1)} %copy-done, f32[1024,2048]{1,0:T(8,128)} %logsum.1.rows_ref, ...), custom_call_target="tpu_custom_call" | custom-call | tf_op jit(solution)/shard_map/trips/pallas_call | solution.py:226
  (13 shorter events, 0.1 us)
Async XLA Ops:
  2.3 10.1 %all-to-all-start = ((s32[8,1,32]{2,1,0:T(1,128)}), s32[8,1,32]{2,1,0:T(1,128)S(1)}, u32[]{:S(2)}, u32[]{:S(2)}) async-start(s32[8,1,32]{2,1,0:T(1,128)} %all_to_all.9), calls=%async_computation | async-start | bytes 8192 | tf_op jit(solution)/shard_map/all_to_all | solution.py:274
  10.0 8.5 %copy-start.2 = (f32[8,8,16]{2,1,0:T(8,128)S(1)}, f32[8,8,16]{2,1,0:T(8,128)}, u32[]{:S(2)}) copy-start(f32[8,8,16]{2,1,0:T(8,128)} %param.12) | copy-start | bytes 12292
  10.0 8.6 %copy-start.4 = (s32[12]{0:T(128)S(1)}, s32[12]{0:T(128)}, u32[]{:S(2)}) copy-start(s32[12]{0:T(128)} %param.16) | copy-start | bytes 148
  10.1 8.8 %copy-start.3 = (f32[12,8]{0,1:T(8,128)S(1)}, f32[12,8]{0,1:T(8,128)}, u32[]{:S(2)}) copy-start(f32[12,8]{0,1:T(8,128)} %param.13) | copy-start | bytes 1156
  12.4 120.2 %all-to-all-start.1 = ((bf16[8,1024,128]{2,1,0:T(8,128)(2,1)}), bf16[8,1024,128]{2,1,0:T(8,128)(2,1)S(1)}, u32[]{:S(2)}, u32[]{:S(2)}) async-start(bf16[8,1024,128]{2,1,0:T(8,128)(2,1)} %reshape.82), calls=%async_computation.1 | async-start | bytes 4194304 | tf_op jit(solution)/shard_map/all_to_all | solution.py:271
  48.3 6.9 %copy-start.5 = (f32[12]{0:T(128)S(1)}, f32[12]{0:T(128)}, u32[]{:S(2)}) copy-start(f32[12]{0:T(128)} %param.14) | copy-start | bytes 148
  48.3 7.1 %copy-start.1 = (f32[4]{0:T(128)S(1)}, f32[4]{0:T(128)}, u32[]{:S(2)}) copy-start(f32[4]{0:T(128)} %theta_ref.1) | copy-start | bytes 52
  57.3 75.4 %copy-start = (bf16[128,2048]{1,0:T(8,128)(2,1)S(1)}, bf16[128,2048]{1,0:T(8,128)(2,1)}, u32[]{:S(2)}) copy-start(bf16[128,2048]{1,0:T(8,128)(2,1)} %attr_ref.3) | copy-start | bytes 1572868

commit v2 on v1

v2 whole, which is shorter than its diff:
```python
import functools
import math

import jax
import jax.numpy as jnp
from jax import lax
from jax.experimental import pallas as pl
from jax.experimental.pallas import tpu as pltpu
from jax.sharding import PartitionSpec as P

LOG2E = math.log2(math.e)
LN2 = math.log(2.0)
ROWS = 16
STEP_BLOCKS = 16
NS = 2


def logsum_kernel(
    keep_ref, inv_ref, theta_ref, end_ref, skim_ref, coef_ref, const_ref, mconst_ref, scale_ref, out_ref, *scratch
):
    tables, block_rows, width = skim_ref.shape
    modes = coef_ref.shape[0]
    nests = theta_ref.shape[0]
    w_refs, acc_refs = scratch[:NW], scratch[NW:]
    rows = HALF
    narrow = tables * rows
    row_id = lax.broadcasted_iota(jnp.int32, (rows, narrow), 0)
    lane_id = lax.broadcasted_iota(jnp.int32, (rows, narrow), 1)
    diagonal = lax.rem(lane_id, rows) == row_id
    groups = block_rows // rows
    pair = PAIR

    def build(index, w_scratch):
        rest = coef_ref[...] * scale_ref[0, pl.ds(index, 1), :]
        pieces = []
        for piece in range(NP):
            rounded = rest.astype(jnp.bfloat16).astype(jnp.float32)
            rest = rest - rounded
            pieces.append(rounded)
        if CONST:
            pieces.append(const_ref[...])
        for mode in range(0, modes, 16 // rows):
            strips = []
            for piece, value in enumerate(pieces):
                tiles = []
                for sub in range(16 // rows):
                    tile = jnp.broadcast_to(value[mode + sub:mode + sub + 1, :], (rows, narrow))
                    tiles.append(jnp.where(diagonal, tile, 0.0) if piece < NP else tile)
                strips.append(tiles[0] if len(tiles) == 1 else jnp.concatenate(tiles, axis=0))
            strip = jnp.concatenate(strips, axis=1).astype(jnp.bfloat16)
            w_scratch[mode * rows:mode * rows + 16, :] = strip

    def multiply(index, w_scratch, start):
        cols = pl.ds(pl.multiple_of(index * 128, 128), 128)
        parts = []
        for group in range(start * rows // ROWS, (start + pair) * rows // ROWS):
            wide = skim_ref[:, group * ROWS:(group + 1) * ROWS, cols].astype(jnp.float32)
            parts.append(wide[:, :rows].reshape(narrow, 128).astype(jnp.bfloat16))
            parts.append(wide[:, rows:].reshape(narrow, 128).astype(jnp.bfloat16))
        data = jnp.concatenate(parts, axis=1)
        pieces = [data] * NP + [jnp.ones((narrow, 128 * pair), jnp.bfloat16)]
        return jnp.dot(w_scratch[...], jnp.concatenate(pieces, axis=0), preferred_element_type=jnp.float32)

    def finish(index, start, util):
        cols = pl.ds(pl.multiple_of(index * 128, 128), 128)
        for offset in range(pair):
            acc_ref = acc_refs[(start + offset) % len(acc_refs)]
            part = util[:, offset * 128:(offset + 1) * 128].reshape(modes, rows, 128)
            top = part[0]
            for mode in range(1, modes):
                top = jnp.maximum(top, part[mode])
            acc = None
            for mode in range(modes):
                term = jnp.exp2((part[mode] - top) * inv_ref[mode])
                acc = term if acc is None else term + keep_ref[mode] * acc
                acc_ref[mode] = acc
            total = None
            for nest in range(nests):
                nest_sum = jnp.maximum(acc_ref[end_ref[nest]], 1.2e-38)
                value = jnp.exp2(theta_ref[nest] * jnp.log(nest_sum))
                total = value if total is None else total + value
            group = start + offset
            out_ref[group * rows:(group + 1) * rows, cols] = top * LN2 + jnp.log(total)

    copies = len(w_refs)

    def column_blocks(index, carry):
        for copy in range(copies):
            build(index * copies + copy, w_refs[copy])
        pending = []
        for copy in range(copies):
            for start in range(0, groups, pair):
                block = index * copies + copy
                pending.append((block, start, multiply(block, w_refs[copy], start)))
                if len(pending) > AHEAD:
                    finish(*pending.pop(0))
        for item in pending:
            finish(*item)
        return carry

    lax.fori_loop(0, width // 128 // copies, column_blocks, 0)


HALF = 8
NP = 3
CONST = True
NW = 2
AHEAD = 1
PAIR = 2
NACC = 8


def nest_logsum(skim_part, scale_part, mode_coef, mode_const, nest_theta, mode_nest):
    tables, row_count, col_count = skim_part.shape
    row_blocks = scale_part.shape[1]
    col_blocks = scale_part.shape[2]
    block_rows = row_count // row_blocks
    block_cols = col_count // col_blocks
    nests = nest_theta.shape[0]
    modes = mode_coef.shape[0]
    depth = tables * HALF
    mode_ids = jnp.arange(modes)
    before = (mode_nest[None, :] < mode_nest[:, None]) | (
        (mode_nest[None, :] == mode_nest[:, None]) & (mode_ids[None, :] < mode_ids[:, None])
    )
    rank = jnp.sum(before.astype(jnp.int32), axis=1)
    place = rank[None, :] == mode_ids[:, None]
    lanes = jnp.arange(depth)
    of_lane = jnp.arange(tables)[:, None] == lanes[None, :] // HALF
    coef = jnp.sum(jnp.where(place[:, :, None], mode_coef[None], 0.0), axis=1) * LOG2E
    coef_wide = jnp.sum(jnp.where(of_lane[None], coef[:, :, None], 0.0), axis=1)
    const = jnp.sum(jnp.where(place, mode_const[None], 0.0), axis=1) * LOG2E
    nest = jnp.sum(jnp.where(place, mode_nest[None], 0), axis=1)
    inverse = jnp.sum(
        jnp.where(nest[:, None] == jnp.arange(nests)[None, :], 1.0 / nest_theta[None, :], 0.0), axis=1
    )
    keep = jnp.concatenate([jnp.zeros((1,), jnp.float32), (nest[1:] == nest[:-1]).astype(jnp.float32)])
    ends = jnp.sum((mode_nest[None, :] <= jnp.arange(nests)[:, None]).astype(jnp.int32), axis=1) - 1
    scale_wide = jnp.sum(jnp.where(of_lane[:, None, None, :], scale_part[:, :, :, None], 0.0), axis=0)
    const_wide = jnp.zeros((modes, depth), jnp.float32)
    rest = const
    for index in range(3):
        piece = lax.reduce_precision(rest, 8, 7)
        rest = rest - piece
        const_wide = jnp.where(lanes[None, :] == index, piece[:, None], const_wide)
    width = min(col_count, 1024)
    per = width // block_cols
    smem = pl.BlockSpec(memory_space=pltpu.SMEM)
    return pl.pallas_call(
        logsum_kernel,
        grid=(row_blocks, col_count // width),
        out_shape=jax.ShapeDtypeStruct((row_count, col_count), jnp.float32),
        in_specs=[
            smem, smem, smem, smem,
            pl.BlockSpec((tables, block_rows, width), lambda i, j: (0, i, j)),
            pl.BlockSpec((modes, depth), lambda i, j: (0, 0)),
            pl.BlockSpec((modes, depth), lambda i, j: (0, 0)),
            smem,
            pl.BlockSpec((1, per, depth), lambda i, j: (i, j, 0)),
        ],
        out_specs=pl.BlockSpec((block_rows, width), lambda i, j: (i, j)),
        scratch_shapes=[pltpu.VMEM((modes * HALF, (NP + CONST) * depth), jnp.bfloat16)] * NW
        + [pltpu.VMEM((modes, HALF, 128), jnp.float32)] * NACC,
        compiler_params=pltpu.CompilerParams(vmem_limit_bytes=40 * 1024 * 1024),
        cost_estimate=pl.CostEstimate(
            flops=200 * row_count * col_count,
            bytes_accessed=(2 * tables + 4) * row_count * col_count,
            transcendentals=21 * row_count * col_count,
        ),
        name="logsum",
    )(keep, inverse, nest_theta * LOG2E, ends, skim_part, coef_wide, const_wide, const, scale_wide)


def stats_kernel(zone_ref, coef_ref, feat_ref, attr_ref, rows_ref, out_ref, top_ref, sum_ref, *score_refs):
    tours = feat_ref.shape[0]
    width = rows_ref.shape[1]
    tour_size = tours // STEP_BLOCKS
    step = pl.program_id(0)
    factor = coef_ref[0] * LOG2E
    half = tours // len(score_refs)
    for index, score_ref in enumerate(score_refs):
        score_ref[...] = jnp.dot(
            feat_ref[index * half:(index + 1) * half, :], attr_ref[...], preferred_element_type=jnp.float32
        )
    for block in range(STEP_BLOCKS):
        home = rows_ref[pl.ds(zone_ref[step * STEP_BLOCKS + block], 1), :] * factor
        for start in range(0, tour_size, ROWS):
            base = block * tour_size + start
            score_ref = score_refs[base // half]
            score = score_ref[base % half:base % half + ROWS, :] * LOG2E + home
            tiles = [score[:, col:col + 128] for col in range(0, width, 128)]
            top = functools.reduce(jnp.maximum, tiles)
            total = functools.reduce(jnp.add, [jnp.exp2(tile - top) for tile in tiles])
            top_ref[base:base + ROWS, :] = top
            sum_ref[base:base + ROWS, :] = total
    for part in range(tours // 128):
        tops = jnp.transpose(top_ref[part * 128:(part + 1) * 128, :])
        sums = jnp.transpose(sum_ref[part * 128:(part + 1) * 128, :])
        top = jnp.max(tops, axis=0, keepdims=True)
        out_ref[0, part:part + 1, :] = top + jnp.log2(jnp.sum(sums * jnp.exp2(tops - top), axis=0, keepdims=True))


def trips_kernel(
    zone_ref, count_ref, coef_ref, feat_ref, attr_ref, rows_ref, parts_ref, out_ref, bias_ref, *score_refs, scale
):
    tours = feat_ref.shape[0]
    tour_size = tours // STEP_BLOCKS
    step = pl.program_id(0)
    width = out_ref.shape[1]
    factor = coef_ref[0] * LOG2E

    @pl.when(step == 0)
    def _():
        out_ref[...] = jnp.zeros_like(out_ref)

    half = tours // len(score_refs)
    for index, score_ref in enumerate(score_refs):
        score_ref[...] = jnp.dot(
            feat_ref[index * half:(index + 1) * half, :], attr_ref[...], preferred_element_type=jnp.float32
        )
    parts = parts_ref[:, 0]
    top = jnp.max(parts, axis=0)
    lse = top + jnp.log2(jnp.sum(jnp.exp2(parts - top[None]), axis=0))
    for part in range(tours // 128):
        bias_ref[part * 128:(part + 1) * 128, :] = jnp.transpose(
            jnp.broadcast_to(lse[part:part + 1, :], (128, 128))
        )
    row_id = lax.broadcasted_iota(jnp.int32, (tour_size, 128), 0)
    for block in range(STEP_BLOCKS):
        zone = zone_ref[step * STEP_BLOCKS + block]
        count = count_ref[step * STEP_BLOCKS + block]
        home = rows_ref[pl.ds(zone, 1), :] * factor
        base = block * tour_size
        bias = jnp.where(row_id < count, bias_ref[base:base + tour_size, :], 1e30)
        totals = []
        for col in range(0, width, 128):
            score = score_refs[base // half][base % half:base % half + tour_size, col:col + 128] * LOG2E + home[:, col:col + 128]
            totals.append(jnp.sum(jnp.exp2(score - bias), axis=0, keepdims=True))
        total = jnp.concatenate(totals, axis=1)
        out_ref[pl.ds(zone, 1), :] = out_ref[pl.ds(zone, 1), :] + scale * total


def tour_trips(feats, logsums, zones, counts, zone_attr, logsum_coef, scale):
    tours, features = feats.shape
    slots = zones.shape[0]
    anchors, width = logsums.shape
    steps = slots // STEP_BLOCKS
    group = tours // steps
    smem = pl.BlockSpec(memory_space=pltpu.SMEM)
    once = pl.Buffered(1)
    common = [
        pl.BlockSpec((group, features), lambda i: (i, 0)),
        pl.BlockSpec((features, width), lambda i: (0, 0), pipeline_mode=once),
        pl.BlockSpec((anchors, width), lambda i: (0, 0), pipeline_mode=once),
    ]
    params = pltpu.CompilerParams(vmem_limit_bytes=48 * 1024 * 1024)
    lines = group // 128
    local_lse = pl.pallas_call(
        stats_kernel,
        grid=(steps,),
        out_shape=jax.ShapeDtypeStruct((steps, lines, 128), jnp.float32),
        in_specs=[smem, smem] + common,
        out_specs=pl.BlockSpec((1, lines, 128), lambda i: (i, 0, 0)),
        scratch_shapes=[
            pltpu.VMEM((group, 128), jnp.float32),
            pltpu.VMEM((group, 128), jnp.float32),
        ]
        + [pltpu.VMEM((group // NS, width), jnp.float32)] * NS,
        compiler_params=params,
        name="stats",
    )(zones, logsum_coef, feats, zone_attr, logsums)
    gathered = lax.all_gather(local_lse, "dest")
    return pl.pallas_call(
        functools.partial(trips_kernel, scale=scale),
        grid=(steps,),
        out_shape=jax.ShapeDtypeStruct((anchors, width), jnp.float32),
        in_specs=[smem, smem, smem] + common
        + [pl.BlockSpec((gathered.shape[0], 1, lines, 128), lambda i: (0, i, 0, 0))],
        out_specs=pl.BlockSpec((anchors, width), lambda i: (0, 0), pipeline_mode=once),
        scratch_shapes=[pltpu.VMEM((group, 128), jnp.float32)]
        + [pltpu.VMEM((group // NS, width), jnp.float32)] * NS,
        compiler_params=params,
        name="trips",
    )(zones, counts, logsum_coef, feats, zone_attr, logsums, gathered)


def local(
    skim_tables,
    block_scale,
    mode_coef,
    mode_const,
    nest_theta,
    mode_nest,
    logsum_coef,
    tour_attr,
    zone_attr,
    block_zone,
    block_count,
):
    sources = lax.axis_size("orig")
    blocks_here = block_zone.shape[0]
    anchors = skim_tables.shape[1]
    tour_size = tour_attr.shape[0] // blocks_here
    features = tour_attr.shape[1]
    capacity = max(2, 2 * blocks_here // sources)
    slot_count = sources * capacity
    factor = anchors * sources / tour_size
    source_dev = block_zone // anchors
    local_zone = block_zone - source_dev * anchors
    block_ids = jnp.arange(blocks_here)
    same = (source_dev[:, None] == source_dev[None, :]) & (block_ids[None, :] < block_ids[:, None])
    slot_rank = jnp.sum(same.astype(jnp.int32), axis=1)
    slot_of_block = source_dev * capacity + slot_rank
    slot_match = slot_of_block[None, :] == jnp.arange(slot_count)[:, None]
    code = local_zone * 64 + block_count
    send_code = jnp.sum(jnp.where(slot_match, code[None, :], 0), axis=1)
    tour_feats = tour_attr.reshape(blocks_here, tour_size * features)
    send_feats = jnp.dot(slot_match.astype(jnp.bfloat16), tour_feats)
    recv_feats = lax.all_to_all(
        send_feats.reshape(sources, capacity * tour_size, features), "orig", split_axis=0, concat_axis=0, tiled=True
    )
    recv_code = lax.all_to_all(
        send_code.reshape(sources, capacity), "orig", split_axis=0, concat_axis=0, tiled=True
    ).reshape(slot_count)
    logsums = nest_logsum(skim_tables, block_scale, mode_coef, mode_const, nest_theta, mode_nest)
    trip_matrix = tour_trips(
        recv_feats.reshape(slot_count * tour_size, features),
        logsums,
        recv_code // 64,
        recv_code % 64,
        zone_attr,
        logsum_coef,
        factor,
    )
    return (logsums, trip_matrix)


def solution(mesh):
    return jax.shard_map(
        local,
        mesh=mesh,
        in_specs=(
            P(None, "orig", "dest"),
            P(None, "orig", "dest"),
            P(),
            P(),
            P(),
            P(),
            P(),
            P("orig", None),
            P(None, "dest"),
            P("orig"),
            P("orig"),
        ),
        out_specs=(P("orig", "dest"), P("orig", "dest")),
        check_vma=False,
    )
```

time: 280 us -> 139 us (0.50)
  Pallas kernels: 215 us -> 110 us
  local copies, waits for them, and re-layouts: 39.8 us -> 5.23 us
    pallas_call x1, Pallas kernels: 97.1 us -> 25.5 us  [tour_trips(): pl.pallas_call(stats_kernel, grid=(steps,), out_shape=jax.ShapeDtypeStruc...]
    another operation x7 -> x0, local copies, waits for them, and re-layouts: 20.6 us -> none  [nest_logsum(): weights = jnp.stack(pieces, axis=2)]
    pallas_call x1, Pallas kernels: 74.1 us -> 55.5 us  [nest_logsum(): pl.pallas_call(logsum_kernel, grid=(row_blocks, col_count // width), out_...]
    pallas_call x1, Pallas kernels: 43.5 us -> 29.1 us  [tour_trips(): pl.pallas_call(functools.partial(trips_kernel, scale=scale), grid=(steps,...]
    broadcast_in_dim x3 -> x0, local copies, waits for them, and re-layouts: 13.9 us -> none  [nest_logsum(): jnp.repeat(piece, ROWS, axis=-1)]
  transfers between devices with their start and end apart: 2 -> 2, of which waited for: 0 -> 0; matrix products, arithmetic and copies ran while one was open for 16% -> 5% of each run, Pallas kernels for 26% -> 40%
where the time goes in v2:
time: 139 us
  Pallas kernels  110 us (79%)
  starting transfers between devices  11.1 us (8%)
  blocking collectives  7.05 us (5%)
  local copies, waits for them, and re-layouts  5.23 us (4%)
  other arithmetic  2.97 us (2%)
  between operations  1.46 us (1%)
    pallas_call x1, Pallas kernels, nest_logsum(): pl.pallas_call(logsum_kernel, grid=(row_blocks, col_count // width), out_...  55.5 us
    pallas_call x1, Pallas kernels, tour_trips(): pl.pallas_call(functools.partial(trips_kernel, scale=scale), grid=(steps,...  29.1 us
    pallas_call x1, Pallas kernels, tour_trips(): pl.pallas_call(stats_kernel, grid=(steps,), out_shape=jax.ShapeDtypeStruc...  25.5 us
    all_gather x1, blocking collectives, tour_trips(): gathered = lax.all_gather(local_lse, 'dest')  7.05 us
    all_to_all x1, starting transfers between devices, local(): lax.all_to_all(send_feats.reshape(sources, capacity * tour_size, features...  5.58 us
    all_to_all x1, starting transfers between devices, local(): lax.all_to_all(send_code.reshape(sources, capacity), 'orig', split_axis=0...  5.49 us
  transfers between devices with their start and end apart: 2, of which 0 were waited for; matrix products, arithmetic and copies ran while one was open for 5% of the time, Pallas kernels for 40%

profile of v2, /device:TPU:25, one launch (start us, length us, event | category | flops | bytes accessed | tf_op | source)
XLA Modules:
  0.0 138.6 jit_solution(1050307037056923769)
XLA Ops:
  0.6 0.7 multiply_add_fusion
  1.3 0.2 convert_reduce_fusion
  1.5 0.1 select_reduce_fusion.1
  1.6 0.7 all_to_all.9
  2.3 5.5 %all-to-all-start = ((s32[8,1,32]{2,1,0:T(1,128)}), s32[8,1,32]{2,1,0:T(1,128)S(1)}, u32[]{:S(2)}, u32[]{:S(2)}) async-start(s32[8,1,32]{2,1,0:T(1,128)} %all_to_all.9), calls=%async_computation | async-start | bytes 8192 | tf_op jit(solution)/shard_map/all_to_all | solution.py:322
  7.8 1.5 %reshape.155 = bf16[128,4096]{1,0:T(8,128)(2,1)S(1)} reshape(bf16[4096,128]{1,0:T(8,128)(2,1)} %param.18) | data formatting | bytes 2097152 | tf_op jit(solution)/shard_map/reshape | solution.py:317
  9.3 0.7 fusion
  10.0 2.3 %reshape.156 = bf16[8,1024,128]{2,1,0:T(8,128)(2,1)} reshape(bf16[256,4096]{1,0:T(8,128)(2,1)S(1)} %fusion) | data formatting | bytes 4194304 | tf_op jit(solution)/shard_map/reshape | solution.py:320
  12.4 0.0 copy-start.3
  12.4 0.0 copy-start.4
  12.4 0.0 copy-start.2
  12.4 0.0 copy-start.5
  12.4 0.0 copy-start.1
  12.4 0.0 all-to-all-done
  12.4 5.6 %all-to-all-start.1 = ((bf16[8,1024,128]{2,1,0:T(8,128)(2,1)}), bf16[8,1024,128]{2,1,0:T(8,128)(2,1)S(1)}, u32[]{:S(2)}, u32[]{:S(2)}) async-start(bf16[8,1024,128]{2,1,0:T(8,128)(2,1)} %reshape.156), calls=%async_computation.1 | async-start | bytes 4194304 | tf_op jit(solution)/shard_map/all_to_all | solution.py:319
  18.7 0.0 copy-done.3
  18.7 0.2 convert_reduce_fusion.1
  18.9 0.1 select_reduce_fusion.5
  19.0 0.1 slice_compare_fusion
  19.0 0.1 add_convert_fusion.keep_ref
  19.1 0.1 convert_reduce_fusion.2
  19.2 0.0 copy-done.4
  19.3 0.1 select_reduce_fusion.4
  19.4 0.0 copy-done.2
  19.4 0.1 select_reduce_fusion.3
  19.5 0.0 copy-done.5
  19.5 0.1 select_reduce_fusion.6.inv_ref
  19.6 0.1 select_reduce_fusion.2.coef_ref
  19.7 0.0 copy-done.1
  19.7 0.2 select_reduce_fusion.scale_ref
  19.9 0.1 select_select_fusion.const_ref
  20.0 0.0 copy-start
  20.0 55.5 %logsum.1.rows_ref = f32[1024,2048]{1,0:T(8,128)} custom-call(f32[12]{0:T(128)S(1)} %add_convert_fusion.keep_ref, f32[12]{0:T(128)S(1)} %select_reduce_fusion.6.inv_ref, f32[4]{0:T(128)S(1)} %get-tuple-element.10.theta_ref, s32[4]{0:T(128)S(1)} %broadcast_add_fusion.end_ref, bf16[8,1024,2048]{2,1,0:T(8,128)(2,1)} %skim_ref.1, ...), custom_call_target="tpu_custom_call" | custom-call | flops 419430400 | bytes 41943040 | tf_op jit(solution)/shard_map/logsum/pallas_call | solution.py:149
  75.6 0.6 broadcast.195
  76.1 0.7 reduce.3
  76.9 0.1 reshape.154
  76.9 0.0 all-to-all-done.1
  77.0 0.0 copy-done
  77.0 25.5 %stats.1 = f32[16,4,128]{2,1,0:T(4,128)S(1)} custom-call(s32[256]{0:T(256)S(1)} %get-tuple-element.5.zone_ref, f32[1]{0:T(128)S(6)} %copy.15.coef_ref, bf16[8192,128]{1,0:T(8,128)(2,1)S(1)} %bitcast.3, bf16[128,2048]{1,0:T(8,128)(2,1)S(1)} %copy-done, f32[1024,2048]{1,0:T(8,128)} %logsum.1.rows_ref), custom_call_target="tpu_custom_call" | custom-call | tf_op jit(solution)/shard_map/stats/pallas_call | solution.py:258
  102.5 7.1 %all-gather = f32[64,4,128]{2,1,0:T(4,128)S(1)} all-gather(f32[16,4,128]{2,1,0:T(4,128)S(1)} %stats.1), channel_id=2, replica_groups=mesh['orig'=8,'dest'=4] {'dest'}, dimensions={0}, use_global_device_ids=true | all-gather | bytes 163840 | tf_op jit(solution)/shard_map/all_gather | solution.py:272
  109.5 29.1 %trips.1 = f32[1024,2048]{1,0:T(8,128)} custom-call(s32[256]{0:T(256)S(1)} %get-tuple-element.5.zone_ref, s32[256]{0:T(256)S(1)} %get-tuple-element.4.count_ref, f32[1]{0:T(128)S(6)} %copy.15.coef_ref, bf16[8192,128]{1,0:T(8,128)(2,1)S(1)} %bitcast.4, bf16[128,2048]{1,0:T(8,128)(2,1)S(1)} %copy-done, f32[1024,2048]{1,0:T(8,128)} %logsum.1.rows_ref, ...), custom_call_target="tpu_custom_call" | custom-call | tf_op jit(solution)/shard_map/trips/pallas_call | solution.py:273
  (11 shorter events, 0.1 us)
Async XLA Ops:
  2.3 10.1 %all-to-all-start = ((s32[8,1,32]{2,1,0:T(1,128)}), s32[8,1,32]{2,1,0:T(1,128)S(1)}, u32[]{:S(2)}, u32[]{:S(2)}) async-start(s32[8,1,32]{2,1,0:T(1,128)} %all_to_all.9), calls=%async_computation | async-start | bytes 8192 | tf_op jit(solution)/shard_map/all_to_all | solution.py:322
  12.4 6.3 %copy-start.3 = (s32[12]{0:T(128)S(1)}, s32[12]{0:T(128)}, u32[]{:S(2)}) copy-start(s32[12]{0:T(128)} %param.16) | copy-start | bytes 148
  12.4 6.9 %copy-start.4 = (f32[12]{0:T(128)S(1)}, f32[12]{0:T(128)}, u32[]{:S(2)}) copy-start(f32[12]{0:T(128)} %param.14) | copy-start | bytes 148
  12.4 7.0 %copy-start.2 = (f32[12,8]{0,1:T(8,128)S(1)}, f32[12,8]{0,1:T(8,128)}, u32[]{:S(2)}) copy-start(f32[12,8]{0,1:T(8,128)} %param.13) | copy-start | bytes 1156
  12.4 7.1 %copy-start.5 = (f32[4]{0:T(128)S(1)}, f32[4]{0:T(128)}, u32[]{:S(2)}) copy-start(f32[4]{0:T(128)} %param.15) | copy-start | bytes 52
  12.4 7.3 %copy-start.1 = (f32[8,8,16]{2,1,0:T(8,128)S(1)}, f32[8,8,16]{2,1,0:T(8,128)}, u32[]{:S(2)}) copy-start(f32[8,8,16]{2,1,0:T(8,128)} %param.12) | copy-start | bytes 12292
  12.4 64.5 %all-to-all-start.1 = ((bf16[8,1024,128]{2,1,0:T(8,128)(2,1)}), bf16[8,1024,128]{2,1,0:T(8,128)(2,1)S(1)}, u32[]{:S(2)}, u32[]{:S(2)}) async-start(bf16[8,1024,128]{2,1,0:T(8,128)(2,1)} %reshape.156), calls=%async_computation.1 | async-start | bytes 4194304 | tf_op jit(solution)/shard_map/all_to_all | solution.py:319
  20.0 56.9 %copy-start = (bf16[128,2048]{1,0:T(8,128)(2,1)S(1)}, bf16[128,2048]{1,0:T(8,128)(2,1)}, u32[]{:S(2)}) copy-start(bf16[128,2048]{1,0:T(8,128)(2,1)} %attr_ref.3) | copy-start | bytes 1572868
